TPU v7x, 32 devices: a whole 2x2x4 slice. The times are simulated.
32 devices in a mesh: layer: 4 (over z), col: 8 (over y, x, core).
Axes of the slice: x: 2, y: 2, z: 4, core: 2. Of those that a mesh axis runs over, the one named last changes fastest.
Arguments:
- factors: bfloat16 [4, 8, 2048, 64], P('layer', 'col'), may hold values from -0.9 to 0.9
- cores: float32 [4, 64, 64], P('layer'), may hold values from -2 to 6, as said below
- tile_list: int32 [64, 2], P('col'), may hold values from 0 to 7, as said below
- probes: bfloat16 [2048, 64, 64], P(None, 'col'), may hold values from -6 to 6
Outputs:
- basis: float32 [2048, 64, 64], P('layer', 'col')
- update_right: float32 [2048, 64, 64], P('layer', 'col')
Inputs may be any that keep to these rules, and one draw needn't show every extreme that they name: `tile_list`: each row is a block row and a block column of a tile of the lower triangle: the first is not below the second. `cores`: each matrix is symmetric positive definite: a Gram matrix plus a positive diagonal.
All inputs are finite; a program needn't handle non-finite values.
Results may differ from a plain program's by a relative error of at most 0.02.
Values may be sent and summed in bfloat16 or wider, within the bound.
A program may use at most 64 MiB of HBM per device.

v0:
```python
import math

import jax
import jax.numpy as jnp
from jax import lax
from jax.sharding import PartitionSpec as P


def local(factors, cores, tile_list, probes):
    highest = lax.Precision.HIGHEST
    tile_order = probes.shape[0]
    rank = probes.shape[2]
    gathered = lax.all_gather(factors, "col", axis=1, tiled=True)
    left_rows = jnp.take(gathered, tile_list[:, 0], axis=1)
    right_rows = jnp.take(gathered, tile_list[:, 1], axis=1)
    sketch = jnp.einsum("ktbr,bts->ktrs", right_rows, probes, preferred_element_type=jnp.float32)
    core_first = jnp.einsum("kar,ktrs->ktas", cores, sketch, precision=highest).astype(jnp.bfloat16)
    part_sample = jnp.einsum(
        "ktbr,ktrs->bts", left_rows, core_first, preferred_element_type=jnp.float32
    )
    share_rows = tile_order // lax.axis_size("layer")
    row_start = lax.axis_index("layer") * share_rows
    unit_matrix = jnp.eye(rank, dtype=jnp.float32)
    samples = lax.psum(part_sample.astype(jnp.bfloat16), "layer").astype(jnp.float32)
    gram = jnp.einsum("btr,bts->trs", samples, samples, precision=highest)
    chol = jnp.linalg.cholesky(gram)
    chol_inverse = jax.scipy.linalg.solve_triangular(
        chol, jnp.broadcast_to(unit_matrix, chol.shape), lower=True
    )
    ortho = jnp.einsum("btr,tsr->bts", samples, chol_inverse, precision=highest)
    ortho_half = ortho.astype(jnp.bfloat16)
    ortho_local = lax.dynamic_slice_in_dim(ortho, row_start, share_rows, 0)
    projected = jnp.einsum(
        "ktbr,bts->ktrs", left_rows, ortho_half, preferred_element_type=jnp.float32
    )
    core_second = jnp.einsum("kar,ktrs->ktas", cores, projected, precision=highest).astype(
        jnp.bfloat16
    )
    update_right = lax.psum_scatter(
        jnp.einsum(
            "ktbr,ktrs->bts", right_rows, core_second, preferred_element_type=jnp.float32
        ).astype(jnp.bfloat16),
        "layer",
        scatter_dimension=0,
        tiled=True,
    ).astype(jnp.float32)
    basis = ortho_local * math.sqrt(tile_order)
    return (basis, update_right)


def solution(mesh):
    placed = (
        P("layer", "col", None, None),
        P("layer", None, None),
        P("col", None),
        P(None, "col", None),
    )
    return jax.shard_map(
        local,
        mesh=mesh,
        in_specs=placed,
        out_specs=(P("layer", "col", None), P("layer", "col", None)),
        check_vma=False,
    )
```

profile of v0, /device:TPU:0, one launch (start us, length us, event | category | flops | bytes accessed | tf_op | source)
XLA Modules:
  0.0 290.1 jit_solution(2075622981553070402)
XLA Ops:
  7.2 0.0 copy-start
  7.2 0.0 all-gather.2.cloned.1.call-start
  7.2 0.7 all-gather.2.cloned.1.call-update
  7.9 0.0 all-reduce.2.cloned.1.call-start
  8.0 0.8 compare_and_fusion
  8.7 31.8 %all-gather.2.cloned.1.call-done = bf16[1,8,2048,64]{2,3,0,1:T(8,128)(2,1)} async-done(((bf16[1,1,2048,64]{2,3,0,1:T(8,128)(2,1)}), bf16[1,8,2048,64]{2,3,0,1:T(8,128)(2,1)}) %all-gather.2.cloned.1.call-update) | async-done | bytes 2097168 | tf_op jit(solution)/shard_map/all_gather | solution.py:13
  40.5 3.6 %gather_fusion = bf16[8,2048,64]{1,2,0:T(8,128)(2,1)} fusion(bf16[8,2048,64]{1,2,0:T(8,128)(2,1)} %bitcast.90, s32[1024]{0:T(1024)S(1)} %get-tuple-element.10), kind=kCustom, calls=%fused_computation.clone | custom fusion | bytes 4194336 | tf_op jit(solution)/shard_map/jit(_take)/gather | solution.py:15
  44.1 3.6 %gather_fusion.1 = bf16[8,2048,64]{1,2,0:T(8,128)(2,1)} fusion(bf16[8,2048,64]{1,2,0:T(8,128)(2,1)} %bitcast.91, s32[1024]{0:T(1024)S(1)} %get-tuple-element.9), kind=kCustom, calls=%fused_computation.1.clone | custom fusion | bytes 4194336 | tf_op jit(solution)/shard_map/jit(_take)/gather | solution.py:14
  47.7 0.0 copy-done
  47.7 0.0 copy-start.5
  47.7 0.0 copy-start.1
  47.7 2.5 fusion.7
  50.3 0.0 copy-done.5
  50.3 0.4 fusion.15
  50.6 0.0 copy-done.1
  50.6 2.1 fusion
  52.8 0.0 all-reduce.2.cloned.1.call-update
  52.8 0.0 reduce-scatter.2.cloned.1.call-start
  52.9 86.6 %all-reduce.2.cloned.1.call-done = bf16[2048,8,64]{0,2,1:T(8,128)(2,1)} async-done(((bf16[2048,8,64]{0,2,1:T(8,128)(2,1)}), bf16[2048,8,64]{0,2,1:T(8,128)(2,1)}) %all-reduce.2.cloned.1.call-update) | async-done | bytes 2097168 | tf_op jit(solution)/shard_map/psum | solution.py:24
  139.5 2.9 %fusion.28 = f32[8,64,64]{2,1,0:T(8,128)S(1)} fusion(bf16[2048,8,64]{0,2,1:T(8,128)(2,1)} %all-reduce.2.cloned.1.call-done), kind=kOutput, calls=%fused_computation.45 | convolution fusion | flops 134217728 | bytes 2228224 | tf_op jit(solution)/shard_map/btr,bts->trs/dot_general | solution.py:25
  142.4 0.1 copy.11
  142.5 46.9 %custom-call.8 = f32[8,64,64]{2,1,0:T(8,128)S(1)} custom-call(f32[8,64,64]{2,1,0:T(8,128)S(1)} %fusion.19), custom_call_target="Cholesky" | custom-call | tf_op jit(solution)/shard_map/jit(cholesky)/cholesky | solution.py:26
  189.5 0.1 compare_reduce_fusion
  189.6 0.1 select_bitcast_fusion
  189.7 39.3 %custom-call.9 = f32[8,1,64,64]{2,3,1,0:T(8,128)S(1)} custom-call(f32[8,1,64,64]{3,2,1,0:T(8,128)S(1)} %select_bitcast_fusion), custom_call_target="InvertDiagBlocksLowerTriangular" | custom-call | tf_op jit(solution)/shard_map/jit(_solve_triangular)/vmap()/triangular_solve | solution.py:27
  229.0 0.6 fusion.17
  229.7 0.0 copy-start.2
  229.7 3.5 %fusion.29 = f32[8,64,2048]{2,1,0:T(8,128)S(1)} fusion(f32[8,64,64]{2,1,0:T(8,128)S(1)} %fusion.17, bf16[2048,8,64]{0,2,1:T(8,128)(2,1)} %all-reduce.2.cloned.1.call-done), kind=kOutput, calls=%fused_computation.46 | convolution fusion | flops 805306368 | bytes 6422528 | tf_op jit(solution)/shard_map/btr,tsr->bts/dot_general | solution.py:30
  233.2 0.0 copy-done.2
  233.2 0.0 copy-start.3
  233.2 0.0 copy-start.4
  233.2 0.8 fusion.10
  234.0 1.3 copy-done.3
  235.3 0.4 fusion.16
  235.7 0.6 copy-done.4
  236.3 2.1 fusion.1
  238.4 0.0 reduce-scatter.2.cloned.1.call-update
  238.4 2.4 multiply_bitcast_fusion
  240.8 40.6 %reduce-scatter.2.cloned.1.call-done = bf16[512,8,64]{0,2,1:T(8,128)(2,1)} async-done(((bf16[2048,8,64]{0,2,1:T(8,128)(2,1)}), bf16[512,8,64]{0,2,1:T(8,128)(2,1)}) %reduce-scatter.2.cloned.1.call-update) | async-done | bytes 524304 | tf_op jit(solution)/shard_map/reduce_scatter | solution.py:39
  281.4 2.1 convert_element_type.56
  (6 shorter events, 0.1 us)
Async XLA Ops:
  7.2 40.6 %copy-start = (bf16[2048,8,64]{0,2,1:T(8,128)(2,1)S(1)}, bf16[2048,8,64]{0,2,1:T(8,128)(2,1)}, u32[]{:S(2)}) copy-start(bf16[2048,8,64]{0,2,1:T(8,128)(2,1)} %param.9) | copy-start | bytes 6291460
  7.2 33.4 %all-gather.2.cloned.1.call-start = ((), (), s32[]{:S(2)}) async-start(), calls=%async_computation.1 | async-start | bytes 2359296 | tf_op jit(solution)/shard_map/all_gather | solution.py:13
  7.9 131.5 %all-reduce.2.cloned.1.call-start = ((), (), s32[]{:S(2)}) async-start(), calls=%async_computation.2 | async-start | bytes 4194304 | tf_op jit(solution)/shard_map/psum | solution.py:24
  47.7 2.5 copy-start.5
  47.7 2.9 %copy-start.1 = (bf16[8,2048,64]{1,2,0:T(8,128)(2,1)S(1)}, bf16[8,2048,64]{1,2,0:T(8,128)(2,1)}, u32[]{:S(2)}) copy-start(bf16[8,2048,64]{1,2,0:T(8,128)(2,1)} %gather_fusion.1) | copy-start | bytes 6291460
  52.8 228.6 %reduce-scatter.2.cloned.1.call-start = ((), (), s32[]{:S(2)}) async-start(), calls=%async_computation.3 | async-start | bytes 2621440 | tf_op jit(solution)/shard_map/reduce_scatter | solution.py:39
  229.7 3.5 %copy-start.2 = (bf16[8,2048,64]{1,2,0:T(8,128)(2,1)S(1)}, bf16[8,2048,64]{1,2,0:T(8,128)(2,1)}, u32[]{:S(2)}) copy-start(bf16[8,2048,64]{1,2,0:T(8,128)(2,1)} %gather_fusion.1) | copy-start | bytes 6291460
  233.2 2.1 copy-start.3
  233.2 3.1 %copy-start.4 = (bf16[8,2048,64]{1,2,0:T(8,128)(2,1)S(1)}, bf16[8,2048,64]{1,2,0:T(8,128)(2,1)}, u32[]{:S(2)}) copy-start(bf16[8,2048,64]{1,2,0:T(8,128)(2,1)} %gather_fusion) | copy-start | bytes 6291460
Sparse Core Ops, SparseCore 0:
  9.9 30.5 all-gather.1
  52.9 86.5 all-reduce.1
  238.5 42.8 reduce-scatter.1
where the time goes:
time: 290 us
  waiting for transfers between devices  160 us (55%)
  other arithmetic  91.8 us (32%)
  matrix products  15.2 us (5%)
  between operations  13.9 us (5%)
  local copies, waits for them, and re-layouts  9.29 us (3%)
    psum x1, waiting for transfers between devices, local(): lax.psum(part_sample.astype(jnp.bfloat16), 'layer').astype(jnp.float32)  86.6 us
    another operation x4, other arithmetic, local(): chol = jnp.linalg.cholesky(gram)  47.1 us
    reduce_scatter x1, waiting for transfers between devices, local(): lax.psum_scatter(jnp.einsum('ktbr,ktrs->bts', right_rows, core_second, pr...  40.6 us
    another operation x3, other arithmetic, local(): jax.scipy.linalg.solve_triangular(chol, jnp.broadcast_to(unit_matrix, cho...  39.4 us
    all_gather x1, waiting for transfers between devices, local(): gathered = lax.all_gather(factors, 'col', axis=1, tiled=True)  31.8 us
  transfers between devices with their start and end apart: 3, of which 3 were waited for; matrix products, arithmetic and copies ran while one was open for 1% of the time, Pallas kernels for 0%

commit v1 on v0

v1 whole, which is shorter than its diff:
```python
import functools
import math

import jax
import jax.numpy as jnp
from jax import lax
from jax.experimental import pallas as pl
from jax.experimental.pallas import tpu as pltpu
from jax.sharding import PartitionSpec as P

MESH = pl.DeviceIdType.MESH
HIGHEST = lax.Precision.HIGHEST
NN = (((1,), (0,)), ((), ()))
NT = (((1,), (1,)), ((), ()))


def dot(a, b, dims, precision=None):
    return lax.dot_general(a, b, dims, precision=precision, preferred_element_type=jnp.float32)


def invert_factor(gram, rank, count):
    shape = gram.shape
    row = lax.broadcasted_iota(jnp.int32, shape, 0)
    lane = lax.broadcasted_iota(jnp.int32, shape, 1)
    inside = lane % rank
    block = lane // rank
    inverse = jnp.where(row == inside, 1.0, 0.0).astype(jnp.float32)
    pivots = jnp.ones(shape, jnp.float32)
    rest = gram
    for j in range(rank):
        column = jnp.broadcast_to(rest[:, j : j + 1], shape)
        for q in range(1, count):
            at = q * rank + j
            column = jnp.where(block == q, jnp.broadcast_to(rest[:, at : at + 1], shape), column)
        pivot = column[j : j + 1, :]
        pivots = jnp.where(row == j, pivot, pivots)
        if j < rank - 1:
            scale = jnp.where(row > j, column * (1.0 / pivot), 0.0)
            inverse = inverse - scale * inverse[j : j + 1, :]
            rest = rest - scale * rest[j : j + 1, :]
    root = lax.rsqrt(pivots)
    root = root * (1.5 - 0.5 * pivots * root * root)
    return inverse * root


def kernel(nl, nc, tiles_ref, factor_ref, core_ref, probe_ref, basis_ref, right_ref,
           panel, shared, probe, cores, first, sample, gram_out, gram_in, proj_out, proj_in,
           inv, second, sem_local, s_core, r_core, s_panel, r_panel, f_panel, s_rows, r_rows,
           s_shared, f_shared, r_shared, s_first, r_first, s_gram, r_gram, s_proj, r_proj,
           s_inv, r_inv, s_second, r_second):
    l, c = lax.axis_index("layer"), lax.axis_index("col")
    rank, order = factor_ref.shape
    nt = probe_ref.shape[0]
    share = order // nl
    per = -(-nt // nl)
    owners = nt // per
    half = 2 if nc % 2 == 0 else 1
    peers = nc // half
    group, side = c // half, c % half
    other = group * half + (half - 1 - side)

    def at_layer(k):
        return (k, c)

    def at_col(d):
        return (l, d)

    def peer(off):
        return lax.rem(group + off, peers) * half + side

    def next_layer(off):
        return lax.rem(l + off, nl)

    def remote(src, dst, send, recv, device):
        return pltpu.make_async_remote_copy(
            src_ref=src, dst_ref=dst, send_sem=send, recv_sem=recv, device_id=device,
            device_id_type=MESH)

    def when(everyone, pred, body):
        if everyone:
            body()
        else:
            pl.when(pred)(body)

    all_own = owners == nl

    def columns(k):
        return pl.ds(pl.multiple_of(k * share, share), share)

    barrier = pltpu.get_barrier_semaphore()
    for off in range(1, nl):
        pl.semaphore_signal(barrier, inc=1, device_id=at_layer(next_layer(off)), device_id_type=MESH)
    for off in range(1, peers):
        pl.semaphore_signal(barrier, inc=1, device_id=at_col(peer(off)), device_id_type=MESH)
    if half == 2:
        pl.semaphore_signal(barrier, inc=1, device_id=at_col(other), device_id_type=MESH)
    pl.semaphore_wait(barrier, nl - 1 + peers - 1 + half - 1)

    def core_copy(off):
        k = next_layer(off)
        return remote(core_ref, cores.at[l], s_core.at[k], r_core.at[l], at_layer(k))

    def core_arrival(k):
        return remote(core_ref, cores.at[k], s_core.at[k], r_core.at[k], at_layer(k))

    def rows_copy(off):
        k = next_layer(off)
        return remote(factor_ref.at[:, columns(k)], shared.at[c, l], s_rows.at[k], r_rows.at[l],
                      at_layer(k))

    def rows_arrival(k):
        return remote(shared.at[c, k], shared.at[c, k], s_rows.at[k], r_rows.at[k], at_layer(k))

    def panel_copy(off):
        return remote(factor_ref, panel.at[c], s_panel.at[off], r_panel.at[c], at_col(peer(off)))

    def panel_forward(off):
        d = peer(off)
        src = factor_ref if off == 0 else panel.at[d]
        return remote(src, panel.at[d], f_panel.at[off], r_panel.at[d], at_col(other))

    def panel_arrival(d):
        return remote(panel.at[d], panel.at[d], f_panel.at[0], r_panel.at[d], at_col(d))

    def shared_copy(off, k):
        return remote(shared.at[c, k], shared.at[c, k], s_shared.at[off, k], r_shared.at[c, k],
                      at_col(peer(off)))

    def shared_forward(off, k):
        d = peer(off)
        return remote(shared.at[d, k], shared.at[d, k], f_shared.at[off, k], r_shared.at[d, k],
                      at_col(other))

    def shared_arrival(d, k):
        return remote(shared.at[d, k], shared.at[d, k], f_shared.at[0, k], r_shared.at[d, k],
                      at_col(d))

    def exchange(buf_from, buf_to, send, recv, off):
        k = next_layer(off)
        return remote(buf_from(k), buf_to(l), send.at[k], recv.at[l], at_layer(k))

    def arrival(buf_to, send, recv, k):
        return remote(buf_to(k), buf_to(k), send.at[k], recv.at[k], at_layer(k))

    for off in range(1, nl):
        rows_copy(off).start()
    for off in range(1, peers):
        panel_copy(off).start()
    if half == 2:
        panel_forward(0).start()
    for off in range(1, nl):
        core_copy(off).start()
    copies = [
        pltpu.make_async_copy(probe_ref, probe, sem_local.at[0]),
        pltpu.make_async_copy(factor_ref, panel.at[c], sem_local.at[1]),
        pltpu.make_async_copy(factor_ref.at[:, columns(l)], shared.at[c, l], sem_local.at[2]),
        pltpu.make_async_copy(core_ref, cores.at[l], sem_local.at[3]),
    ]
    for copy in copies:
        copy.start()

    for off in range(1, peers):
        panel_arrival(peer(off)).wait_recv()
        if half == 2:
            panel_forward(off).start()

    def send_shared(off, carry):
        k = next_layer(off)
        rows_arrival(k).wait_recv()
        for hop in range(1, peers):
            shared_copy(hop, k).start()
        if half == 2:
            shared_forward(0, k).start()
        return carry

    lax.fori_loop(1, nl, send_shared, 0)
    for copy in copies:
        copy.wait()
    if half == 2:
        for off in range(peers):
            panel_arrival(lax.rem(group + off, peers) * half + (1 - side)).wait_recv()

    local_rows = [
        pltpu.make_async_copy(
            panel.at[lax.rem(c + off, nc), :, columns(l)], shared.at[lax.rem(c + off, nc), l],
            sem_local.at[3 + off])
        for off in range(1, nc)
    ]
    for copy in local_rows:
        copy.start()

    core = cores[l]

    def sketch_pair(p, carry):
        parts = []
        for q in range(2):
            t = 2 * p + q
            block = panel[tiles_ref[1, t]]
            parts.append(dot(probe[t], block, NT))
        pair = dot(jnp.concatenate(parts, axis=0), core, NT, HIGHEST)
        pair = pair.astype(jnp.bfloat16)
        first[l, p] = jnp.concatenate([pair[:rank], pair[rank:]], axis=1)
        return carry

    lax.fori_loop(0, nt // 2, sketch_pair, 0)
    for off in range(1, nl):
        exchange(lambda k: first.at[l], lambda k: first.at[k], s_first, r_first, off).start()

    def pass_shared(off, carry):
        k = next_layer(off)
        for hop in range(1, peers):
            shared_arrival(peer(hop), k).wait_recv()
            if half == 2:
                shared_forward(hop, k).start()
        return carry

    lax.fori_loop(1, nl, pass_shared, 0)
    if half == 2:
        def last_shared(off, carry):
            k = next_layer(off)
            for hop in range(peers):
                shared_arrival(lax.rem(group + hop, peers) * half + (1 - side), k).wait_recv()
            return carry

        lax.fori_loop(1, nl, last_shared, 0)
    for copy in local_rows:
        copy.wait()
    for off in range(1, nl):
        arrival(lambda k: first.at[k], s_first, r_first, next_layer(off)).wait_recv()

    for t in range(nt):
        p, q = t // 2, t % 2
        stack = jnp.concatenate(
            [first[k, p][:, q * rank : (q + 1) * rank] for k in range(nl)], axis=1)
        block = shared[tiles_ref[0, t]].reshape(nl * rank, share)
        rows = dot(stack, block, NN)
        sample[t] = rows
        to, slot = t // per, t % per
        gram_out[to, :, slot * rank : (slot + 1) * rank] = dot(rows, rows, NT, HIGHEST)
    for off in range(1, nl):
        def send_gram(off=off):
            exchange(lambda k: gram_out.at[k], lambda k: gram_in.at[k], s_gram, r_gram, off).start()
        when(all_own, next_layer(off) < owners, send_gram)
    for t in range(nt):
        block = shared[tiles_ref[0, t]].reshape(nl * rank, share)
        rows = sample[t]
        high = rows.astype(jnp.bfloat16)
        low = (rows - high.astype(jnp.float32)).astype(jnp.bfloat16)
        total = dot(high, block, NT) + dot(low, block, NT)
        proj_out[t // per, t % per] = total.astype(jnp.bfloat16)
    for off in range(1, nl):
        def send_proj(off=off):
            exchange(lambda k: proj_out.at[k], lambda k: proj_in.at[k], s_proj, r_proj, off).start()
        when(all_own, next_layer(off) < owners, send_proj)

    def own_tiles():
        gram = gram_out[l]
        for off in range(1, nl):
            k = next_layer(off)
            arrival(lambda k: gram_in.at[k], s_gram, r_gram, k).wait_recv()
            gram = gram + gram_in[k]
        inverse = invert_factor(gram, rank, per)
        inv[l] = inverse
        for off in range(1, nl):
            exchange(lambda k: inv.at[l], lambda k: inv.at[k], s_inv, r_inv, off).start()
        for off in range(1, nl):
            arrival(lambda k: proj_in.at[k], s_proj, r_proj, next_layer(off)).wait_recv()
        for off in range(1, nl):
            core_arrival(next_layer(off)).wait_recv()
        projected = []
        for slot in range(per):
            total = proj_out[l, slot].astype(jnp.float32)
            for off in range(1, nl):
                total = total + proj_in[next_layer(off), slot].astype(jnp.float32)
            projected.append(
                dot(inverse[:, slot * rank : (slot + 1) * rank], total, NN, HIGHEST))
        for k in range(nl):
            piece = jnp.concatenate(
                [x[:, k * rank : (k + 1) * rank] for x in projected], axis=0)
            piece = dot(piece, cores[k], NT, HIGHEST).astype(jnp.bfloat16)
            for slot in range(per):
                second[l, slot, :, k * rank : (k + 1) * rank] = piece[
                    slot * rank : (slot + 1) * rank]
        for off in range(1, nl):
            exchange(lambda k: second.at[l], lambda k: second.at[k], s_second, r_second, off).start()

    when(all_own, l < owners, own_tiles)

    for off in range(1, nl):
        def take_inverse(off=off):
            arrival(lambda k: inv.at[k], s_inv, r_inv, next_layer(off)).wait_recv()
        when(all_own, next_layer(off) < owners, take_inverse)
    scale = math.sqrt(order)
    for t in range(nt):
        slot = t % per
        inverse = inv[t // per][:, slot * rank : (slot + 1) * rank]
        basis_ref[t] = dot(inverse, sample[t], NN, HIGHEST) * scale
    for off in range(1, nl):
        def take_second(off=off):
            arrival(lambda k: second.at[k], s_second, r_second, next_layer(off)).wait_recv()
        when(all_own, next_layer(off) < owners, take_second)
    for t in range(nt):
        block = shared[tiles_ref[1, t]].reshape(nl * rank, share)
        right_ref[t] = dot(second[t // per, t % per], block, NN)

    for off in range(1, nl):
        core_copy(off).wait_send()
        rows_copy(off).wait_send()
        exchange(lambda k: first.at[l], lambda k: first.at[k], s_first, r_first, off).wait_send()

        def sent_sums(off=off):
            exchange(lambda k: gram_out.at[k], lambda k: gram_in.at[k], s_gram, r_gram,
                     off).wait_send()
            exchange(lambda k: proj_out.at[k], lambda k: proj_in.at[k], s_proj, r_proj,
                     off).wait_send()
        when(all_own, next_layer(off) < owners, sent_sums)

        def sent_results(off=off):
            exchange(lambda k: inv.at[l], lambda k: inv.at[k], s_inv, r_inv, off).wait_send()
            exchange(lambda k: second.at[l], lambda k: second.at[k], s_second, r_second,
                     off).wait_send()
        when(all_own, l < owners, sent_results)
        if not all_own:
            def unused_cores(off=off):
                core_arrival(next_layer(off)).wait_recv()
            pl.when(l >= owners)(unused_cores)
    for off in range(1, peers):
        panel_copy(off).wait_send()
    if half == 2:
        for off in range(peers):
            panel_forward(off).wait_send()

    def sent_shared(off, carry):
        k = next_layer(off)
        for hop in range(1, peers):
            shared_copy(hop, k).wait_send()
        if half == 2:
            for hop in range(peers):
                shared_forward(hop, k).wait_send()
        return carry

    lax.fori_loop(1, nl, sent_shared, 0)


def local(nl, nc, factors, cores, tile_list, probes):
    order, nt, rank = probes.shape
    share = order // nl
    per = -(-nt // nl)
    factor = jnp.transpose(factors, (0, 1, 3, 2)).reshape(rank, order)
    probe = jnp.transpose(probes, (1, 2, 0))
    f32, bf16 = jnp.float32, jnp.bfloat16
    dma = pltpu.SemaphoreType.DMA
    out = jax.ShapeDtypeStruct((nt, rank, share), f32)
    basis, right = pl.pallas_call(
        functools.partial(kernel, nl, nc),
        out_shape=(out, out),
        in_specs=[
            pl.BlockSpec(memory_space=pltpu.SMEM),
            pl.BlockSpec(memory_space=pl.ANY),
            pl.BlockSpec(memory_space=pl.ANY),
            pl.BlockSpec(memory_space=pl.ANY),
        ],
        out_specs=[pl.BlockSpec(memory_space=pltpu.VMEM)] * 2,
        scratch_shapes=[
            pltpu.VMEM((nc, rank, order), bf16),
            pltpu.VMEM((nc, nl, rank, share), bf16),
            pltpu.VMEM((nt, rank, order), bf16),
            pltpu.VMEM((nl, rank, rank), f32),
            pltpu.VMEM((nl, nt // 2, rank, 2 * rank), bf16),
            pltpu.VMEM((nt, rank, share), f32),
            pltpu.VMEM((nl, rank, per * rank), f32),
            pltpu.VMEM((nl, rank, per * rank), f32),
            pltpu.VMEM((nl, per, rank, nl * rank), bf16),
            pltpu.VMEM((nl, per, rank, nl * rank), bf16),
            pltpu.VMEM((nl, rank, per * rank), f32),
            pltpu.VMEM((nl, per, rank, nl * rank), bf16),
            dma((3 + nc,)),
            dma((nl,)), dma((nl,)),
            dma((nc,)), dma((nc,)), dma((nc,)),
            dma((nl,)), dma((nl,)),
            dma((nc, nl)), dma((nc, nl)), dma((nc, nl)),
            dma((nl,)), dma((nl,)),
            dma((nl,)), dma((nl,)),
            dma((nl,)), dma((nl,)),
            dma((nl,)), dma((nl,)),
            dma((nl,)), dma((nl,)),
        ],
        compiler_params=pltpu.CompilerParams(
            collective_id=0, has_side_effects=True, vmem_limit_bytes=44 * 1024 * 1024),
    )(jnp.transpose(tile_list), factor, cores.reshape(rank, rank), probe)
    return jnp.transpose(basis, (2, 0, 1)), jnp.transpose(right, (2, 0, 1))


def solution(mesh):
    placed = (
        P("layer", "col", None, None),
        P("layer", None, None),
        P("col", None),
        P(None, "col", None),
    )
    return jax.shard_map(
        functools.partial(local, mesh.shape["layer"], mesh.shape["col"]),
        mesh=mesh,
        in_specs=placed,
        out_specs=(P("layer", "col", None), P("layer", "col", None)),
        check_vma=False,
    )
```

time: 290 us -> 60.4 us (0.21)
  waiting for transfers between devices: 160 us -> 0 us
  other arithmetic: 91.8 us -> 0 us
  Pallas kernels: 0 us -> 53.6 us
  matrix products: 15.2 us -> 0 us
  between operations: 13.9 us -> 0.65 us
  local copies, waits for them, and re-layouts: 9.29 us -> 5.91 us
    psum x1 -> x0, waiting for transfers between devices: 86.6 us -> none  [local(): lax.psum(part_sample.astype(jnp.bfloat16), 'layer').astype(jnp.float32)]
    another operation x7 -> x0, other arithmetic: 86.5 us -> none  [the longest x4 47.1 us: local(): chol = jnp.linalg.cholesky(gram)]
    pallas_call x0 -> x1, Pallas kernels: none -> 53.6 us  [local(): pl.pallas_call(functools.partial(kernel, nl, nc), out_shape=(out, out), i...]
    reduce_scatter x1 -> x0, waiting for transfers between devices: 40.6 us -> none  [local(): lax.psum_scatter(jnp.einsum('ktbr,ktrs->bts', right_rows, core_second, pr...]
    all_gather x1 -> x0, waiting for transfers between devices: 31.8 us -> none  [local(): gathered = lax.all_gather(factors, 'col', axis=1, tiled=True)]
    dot_general x8 -> x0, matrix products: 14.6 us -> none  [the longest x1 3.53 us: local(): ortho = jnp.einsum('btr,tsr->bts', samples, chol_inverse, precision=highest)]
    gather x2 -> x0, local copies, waits for them, and re-layouts: 7.2 us -> none  [the longest x1 3.61 us: local(): left_rows = jnp.take(gathered, tile_list[:, 0], axis=1)]
    unnamed x12 -> x10, local copies, waits for them, and re-layouts: 1.97 us -> 5.91 us
  transfers between devices with their start and end apart: 3 -> 0, of which waited for: 3 -> 0; matrix products, arithmetic and copies ran while one was open for 1% -> 0% of each run, Pallas kernels for 0% -> 0%
where the time goes in v1:
time: 60.4 us; the launch traced here: 60.2 us
  Pallas kernels  53.6 us (89%)
  local copies, waits for them, and re-layouts  5.91 us (10%)
  between operations  0.65 us (1%)
    pallas_call x1, Pallas kernels, local(): pl.pallas_call(functools.partial(kernel, nl, nc), out_shape=(out, out), i...  53.6 us
    unnamed x10, local copies, waits for them, and re-layouts  5.91 us

profile of v1, /device:TPU:0, one launch (start us, length us, event | category | flops | bytes accessed | tf_op | source)
XLA Modules:
  0.0 60.2 jit_solution(7892046198156310179)
XLA Ops:
  0.6 0.0 copy-start
  0.6 1.6 %copy-done = bf16[2048,8,64]{0,2,1:T(8,128)(2,1)S(1)} copy-done((bf16[2048,8,64]{0,2,1:T(8,128)(2,1)S(1)}, bf16[2048,8,64]{0,2,1:T(8,128)(2,1)}, u32[]{:S(2)}) %copy-start) | copy-done | bytes 2097176
  2.2 0.0 copy-start.1
  2.2 0.9 %copy-done.1 = bf16[1,1,2048,64]{2,3,1,0:T(8,128)(2,1)S(1)} copy-done((bf16[1,1,2048,64]{2,3,1,0:T(8,128)(2,1)S(1)}, bf16[1,1,2048,64]{2,3,1,0:T(8,128)(2,1)}, u32[]{:S(2)}) %copy-start.1) | copy-done | bytes 262168
  3.2 0.0 copy-start.2
  3.2 0.8 %copy-done.2 = f32[1,64,64]{2,1,0:T(8,128)S(1)} copy-done((f32[1,64,64]{2,1,0:T(8,128)S(1)}, f32[1,64,64]{2,1,0:T(8,128)}, u32[]{:S(2)}) %copy-start.2) | copy-done | bytes 16408
  3.9 0.0 copy-start.3
  3.9 0.7 %copy-done.3 = s32[8,2]{0,1:T(2,128)S(1)} copy-done((s32[8,2]{0,1:T(2,128)S(1)}, s32[8,2]{0,1:T(2,128)}, u32[]{:S(2)}) %copy-start.3) | copy-done | bytes 88
  4.6 53.6 %shard_map.59 = (f32[8,64,512]{2,1,0:T(8,128)S(1)}, f32[8,64,512]{2,1,0:T(8,128)S(1)}) custom-call(s32[2,8]{1,0:T(2,128)S(1)} %bitcast.13, bf16[64,2048]{1,0:T(8,128)(2,1)S(1)} %bitcast.11, f32[64,64]{1,0:T(8,128)S(1)} %bitcast.12, bf16[8,64,2048]{2,1,0:T(8,128)(2,1)S(1)} %bitcast.8), custom_call_target="tpu_custom_call" | custom-call | tf_op jit(solution)/shard_map/pallas_call | solution.py:354
  58.2 1.0 %copy.8 = f32[512,8,64]{0,2,1:T(8,128)} copy(f32[512,8,64]{0,2,1:T(8,128)S(1)} %bitcast.10) | data formatting | bytes 2097152
  59.2 1.0 %copy.9 = f32[512,8,64]{0,2,1:T(8,128)} copy(f32[512,8,64]{0,2,1:T(8,128)S(1)} %bitcast.9) | data formatting | bytes 2097152
Async XLA Ops:
  0.6 1.6 %copy-start = (bf16[2048,8,64]{0,2,1:T(8,128)(2,1)S(1)}, bf16[2048,8,64]{0,2,1:T(8,128)(2,1)}, u32[]{:S(2)}) copy-start(bf16[2048,8,64]{0,2,1:T(8,128)(2,1)} %param.7) | copy-start | bytes 6291460
  2.2 0.9 %copy-start.1 = (bf16[1,1,2048,64]{2,3,1,0:T(8,128)(2,1)S(1)}, bf16[1,1,2048,64]{2,3,1,0:T(8,128)(2,1)}, u32[]{:S(2)}) copy-start(bf16[1,1,2048,64]{2,3,1,0:T(8,128)(2,1)} %param.4) | copy-start | bytes 786436
  3.2 0.8 %copy-start.2 = (f32[1,64,64]{2,1,0:T(8,128)S(1)}, f32[1,64,64]{2,1,0:T(8,128)}, u32[]{:S(2)}) copy-start(f32[1,64,64]{2,1,0:T(8,128)} %param.5) | copy-start | bytes 49156
  3.9 0.7 %copy-start.3 = (s32[8,2]{0,1:T(2,128)S(1)}, s32[8,2]{0,1:T(2,128)}, u32[]{:S(2)}) copy-start(s32[8,2]{0,1:T(2,128)} %param.6) | copy-start | bytes 196

commit v2 on v1

--- a/solution.py
+++ b/solution.py
@@ -18,29 +18,48 @@
     return lax.dot_general(a, b, dims, precision=precision, preferred_element_type=jnp.float32)
 
 
-def invert_factor(gram, rank, count):
-    shape = gram.shape
-    row = lax.broadcasted_iota(jnp.int32, shape, 0)
-    lane = lax.broadcasted_iota(jnp.int32, shape, 1)
-    inside = lane % rank
+def invert_factor(gram, rank, count, width=4, depth=8):
+    lanes = gram.shape[1]
+    row = lax.broadcasted_iota(jnp.int32, gram.shape, 0)
+    lane = lax.broadcasted_iota(jnp.int32, gram.shape, 1)
     block = lane // rank
-    inverse = jnp.where(row == inside, 1.0, 0.0).astype(jnp.float32)
-    pivots = jnp.ones(shape, jnp.float32)
     rest = gram
-    for j in range(rank):
-        column = jnp.broadcast_to(rest[:, j : j + 1], shape)
-        for q in range(1, count):
-            at = q * rank + j
-            column = jnp.where(block == q, jnp.broadcast_to(rest[:, at : at + 1], shape), column)
-        pivot = column[j : j + 1, :]
-        pivots = jnp.where(row == j, pivot, pivots)
-        if j < rank - 1:
-            scale = jnp.where(row > j, column * (1.0 / pivot), 0.0)
-            inverse = inverse - scale * inverse[j : j + 1, :]
-            rest = rest - scale * rest[j : j + 1, :]
-    root = lax.rsqrt(pivots)
-    root = root * (1.5 - 0.5 * pivots * root * root)
-    return inverse * root
+    inverse = jnp.where(row == lane % rank, 1.0, 0.0).astype(jnp.float32)
+    finished = []
+    for base in range(0, rank, depth):
+        height = rank - base
+        shape = (height, lanes)
+        index, place = row[:height], block[:height]
+        pivots = jnp.ones((depth, lanes), jnp.float32)
+        for start in range(0, depth, width):
+            columns = []
+            for a in range(width):
+                at = base + start + a
+                column = jnp.broadcast_to(rest[:, at : at + 1], shape)
+                for q in range(1, count):
+                    at += rank
+                    other = jnp.broadcast_to(rest[:, at : at + 1], shape)
+                    column = jnp.where(place == q, other, column)
+                columns.append(column)
+            for a in range(width):
+                j = start + a
+                pivot = columns[a][j : j + 1, :]
+                pivots = jnp.where(index[:depth] == j, pivot, pivots)
+                scale = jnp.where(index > j, columns[a] * (1.0 / pivot), 0.0)
+                for b in range(a + 1, width):
+                    columns[b] = columns[b] - scale * columns[b][j : j + 1, :]
+                inverse = inverse - scale * inverse[j : j + 1, :]
+                rest = rest - scale * rest[j : j + 1, :]
+        root = lax.rsqrt(pivots)
+        root = root * (1.5 - 0.5 * pivots * root * root)
+        finished.append(inverse[:depth] * root)
+        rest, inverse = rest[depth:], inverse[depth:]
+    return jnp.concatenate(finished, axis=0)
+
+
+def split(x):
+    high = x.astype(jnp.bfloat16)
+    return high, (x - high.astype(jnp.float32)).astype(jnp.bfloat16)
 
 
 def kernel(nl, nc, tiles_ref, factor_ref, core_ref, probe_ref, basis_ref, right_ref,
@@ -233,20 +252,22 @@
         stack = jnp.concatenate(
             [first[k, p][:, q * rank : (q + 1) * rank] for k in range(nl)], axis=1)
         block = shared[tiles_ref[0, t]].reshape(nl * rank, share)
-        rows = dot(stack, block, NN)
-        sample[t] = rows
+        high, low = split(dot(stack, block, NN))
+        both = jnp.concatenate([high, low], axis=0)
+        sample[t] = jnp.concatenate([both, high], axis=0)
         to, slot = t // per, t % per
-        gram_out[to, :, slot * rank : (slot + 1) * rank] = dot(rows, rows, NT, HIGHEST)
+        product = dot(both, both, NT)
+        gram_out[to, :, slot * rank : (slot + 1) * rank] = (
+            product[:rank, :rank] + product[rank:, rank:]
+            + (product[:rank, rank:] + product[rank:, :rank]))
     for off in range(1, nl):
         def send_gram(off=off):
             exchange(lambda k: gram_out.at[k], lambda k: gram_in.at[k], s_gram, r_gram, off).start()
         when(all_own, next_layer(off) < owners, send_gram)
     for t in range(nt):
         block = shared[tiles_ref[0, t]].reshape(nl * rank, share)
-        rows = sample[t]
-        high = rows.astype(jnp.bfloat16)
-        low = (rows - high.astype(jnp.float32)).astype(jnp.bfloat16)
-        total = dot(high, block, NT) + dot(low, block, NT)
+        total = dot(sample[t, : 2 * rank], block, NT)
+        total = total[:rank] + total[rank:]
         proj_out[t // per, t % per] = total.astype(jnp.bfloat16)
     for off in range(1, nl):
         def send_proj(off=off):
@@ -294,7 +315,9 @@
     for t in range(nt):
         slot = t % per
         inverse = inv[t // per][:, slot * rank : (slot + 1) * rank]
-        basis_ref[t] = dot(inverse, sample[t], NN, HIGHEST) * scale
+        high, low = split(inverse * scale)
+        stack = jnp.concatenate([high, high, low], axis=1)
+        basis_ref[t] = dot(stack, sample[t], NN)
     for off in range(1, nl):
         def take_second(off=off):
             arrival(lambda k: second.at[k], s_second, r_second, next_layer(off)).wait_recv()
@@ -356,9 +379,9 @@
         out_shape=(out, out),
         in_specs=[
             pl.BlockSpec(memory_space=pltpu.SMEM),
-            pl.BlockSpec(memory_space=pl.ANY),
-            pl.BlockSpec(memory_space=pl.ANY),
-            pl.BlockSpec(memory_space=pl.ANY),
+            pl.BlockSpec(memory_space=pltpu.HBM),
+            pl.BlockSpec(memory_space=pltpu.HBM),
+            pl.BlockSpec(memory_space=pltpu.HBM),
         ],
         out_specs=[pl.BlockSpec(memory_space=pltpu.VMEM)] * 2,
         scratch_shapes=[
@@ -367,7 +390,7 @@
             pltpu.VMEM((nt, rank, order), bf16),
             pltpu.VMEM((nl, rank, rank), f32),
             pltpu.VMEM((nl, nt // 2, rank, 2 * rank), bf16),
-            pltpu.VMEM((nt, rank, share), f32),
+            pltpu.VMEM((nt, 3 * rank, share), bf16),
             pltpu.VMEM((nl, rank, per * rank), f32),
             pltpu.VMEM((nl, rank, per * rank), f32),
             pltpu.VMEM((nl, per, rank, nl * rank), bf16),
@@ -386,7 +409,7 @@
             dma((nl,)), dma((nl,)),
         ],
         compiler_params=pltpu.CompilerParams(
-            collective_id=0, has_side_effects=True, vmem_limit_bytes=44 * 1024 * 1024),
+            collective_id=0, has_side_effects=True, vmem_limit_bytes=60 * 1024 * 1024),
     )(jnp.transpose(tile_list), factor, cores.reshape(rank, rank), probe)
     return jnp.transpose(basis, (2, 0, 1)), jnp.transpose(right, (2, 0, 1))
 

time: 60.4 us -> 56.8 us (0.940)
  local copies, waits for them, and re-layouts: 5.91 us -> 3.32 us
  Pallas kernels: 53.6 us -> 52.7 us
    unnamed x10 -> x4, local copies, waits for them, and re-layouts: 5.91 us -> 3.32 us
    pallas_call x1, Pallas kernels: 53.6 us -> 52.7 us  [local(): pl.pallas_call(functools.partial(kernel, nl, nc), out_shape=(out, out), i...]
where the time goes in v2:
time: 56.8 us; the launch traced here: 56.7 us
  Pallas kernels  52.7 us (93%)
  local copies, waits for them, and re-layouts  3.32 us (6%)
  between operations  0.65 us (1%)
    pallas_call x1, Pallas kernels, local(): pl.pallas_call(functools.partial(kernel, nl, nc), out_shape=(out, out), i...  52.7 us
    unnamed x4, local copies, waits for them, and re-layouts  3.32 us

profile of v2, /device:TPU:0, one launch (start us, length us, event | category | flops | bytes accessed | tf_op | source)
XLA Modules:
  0.0 56.7 jit_solution(9375315430583317556)
XLA Ops:
  0.6 52.7 %shard_map.59 = (f32[8,64,512]{2,1,0:T(8,128)}, f32[8,64,512]{2,1,0:T(8,128)}) custom-call(s32[2,8]{1,0:T(2,128)} %bitcast.13, bf16[64,2048]{1,0:T(8,128)(2,1)} %bitcast.11, f32[64,64]{1,0:T(8,128)} %bitcast.12, bf16[8,64,2048]{2,1,0:T(8,128)(2,1)} %bitcast.8), custom_call_target="tpu_custom_call" | custom-call | tf_op jit(solution)/shard_map/pallas_call | solution.py:377
  53.3 0.0 copy-start
  53.3 2.4 %copy.8 = f32[512,8,64]{0,2,1:T(8,128)} copy(f32[512,8,64]{0,2,1:T(8,128)} %bitcast.10) | data formatting | bytes 2097152
  55.7 0.0 copy-done
  55.7 1.0 %copy.9 = f32[512,8,64]{0,2,1:T(8,128)} copy(f32[512,8,64]{0,2,1:T(8,128)S(1)} %bitcast.9) | data formatting | bytes 2097152
Async XLA Ops:
  53.3 2.4 %copy-start = (f32[8,64,512]{2,1,0:T(8,128)S(1)}, f32[8,64,512]{2,1,0:T(8,128)}, u32[]{:S(2)}) copy-start(f32[8,64,512]{2,1,0:T(8,128)} %get-tuple-element.5) | copy-start | bytes 3145732

commit v3 on v2

--- a/solution.py
+++ b/solution.py
@@ -18,7 +18,7 @@
     return lax.dot_general(a, b, dims, precision=precision, preferred_element_type=jnp.float32)
 
 
-def invert_factor(gram, rank, count, width=4, depth=8):
+def invert_factor(gram, rank, count, midway, width=4, depth=8):
     lanes = gram.shape[1]
     row = lax.broadcasted_iota(jnp.int32, gram.shape, 0)
     lane = lax.broadcasted_iota(jnp.int32, gram.shape, 1)
@@ -27,6 +27,8 @@
     inverse = jnp.where(row == lane % rank, 1.0, 0.0).astype(jnp.float32)
     finished = []
     for base in range(0, rank, depth):
+        if base == rank // 2:
+            midway()
         height = rank - base
         shape = (height, lanes)
         index, place = row[:height], block[:height]
@@ -280,24 +282,24 @@
             k = next_layer(off)
             arrival(lambda k: gram_in.at[k], s_gram, r_gram, k).wait_recv()
             gram = gram + gram_in[k]
-        inverse = invert_factor(gram, rank, per)
+        inverse = invert_factor(gram, rank, per, send_second)
         inv[l] = inverse
         for off in range(1, nl):
             exchange(lambda k: inv.at[l], lambda k: inv.at[k], s_inv, r_inv, off).start()
+
+    def send_second():
+        for off in range(1, nl):
+            core_arrival(next_layer(off)).wait_recv()
         for off in range(1, nl):
             arrival(lambda k: proj_in.at[k], s_proj, r_proj, next_layer(off)).wait_recv()
-        for off in range(1, nl):
-            core_arrival(next_layer(off)).wait_recv()
-        projected = []
+        totals = []
         for slot in range(per):
             total = proj_out[l, slot].astype(jnp.float32)
             for off in range(1, nl):
                 total = total + proj_in[next_layer(off), slot].astype(jnp.float32)
-            projected.append(
-                dot(inverse[:, slot * rank : (slot + 1) * rank], total, NN, HIGHEST))
+            totals.append(total)
         for k in range(nl):
-            piece = jnp.concatenate(
-                [x[:, k * rank : (k + 1) * rank] for x in projected], axis=0)
+            piece = jnp.concatenate([x[:, k * rank : (k + 1) * rank] for x in totals], axis=0)
             piece = dot(piece, cores[k], NT, HIGHEST).astype(jnp.bfloat16)
             for slot in range(per):
                 second[l, slot, :, k * rank : (k + 1) * rank] = piece[
@@ -307,24 +309,26 @@
 
     when(all_own, l < owners, own_tiles)
 
-    for off in range(1, nl):
-        def take_inverse(off=off):
-            arrival(lambda k: inv.at[k], s_inv, r_inv, next_layer(off)).wait_recv()
-        when(all_own, next_layer(off) < owners, take_inverse)
     scale = math.sqrt(order)
-    for t in range(nt):
-        slot = t % per
-        inverse = inv[t // per][:, slot * rank : (slot + 1) * rank]
-        high, low = split(inverse * scale)
-        stack = jnp.concatenate([high, high, low], axis=1)
-        basis_ref[t] = dot(stack, sample[t], NN)
-    for off in range(1, nl):
-        def take_second(off=off):
-            arrival(lambda k: second.at[k], s_second, r_second, next_layer(off)).wait_recv()
-        when(all_own, next_layer(off) < owners, take_second)
-    for t in range(nt):
-        block = shared[tiles_ref[1, t]].reshape(nl * rank, share)
-        right_ref[t] = dot(second[t // per, t % per], block, NN)
+    for off in range(nl):
+        def finish(off=off):
+            k = next_layer(off)
+            if off > 0:
+                arrival(lambda k: second.at[k], s_second, r_second, k).wait_recv()
+                arrival(lambda k: inv.at[k], s_inv, r_inv, k).wait_recv()
+            for slot in range(per):
+                t = k * per + slot
+                inverse = inv[k][:, slot * rank : (slot + 1) * rank]
+                high, low = split(inverse)
+                raw = second[k, slot]
+                middle = dot(jnp.concatenate([high, low], axis=1),
+                             jnp.concatenate([raw, raw], axis=0), NN).astype(jnp.bfloat16)
+                block = shared[tiles_ref[1, t]].reshape(nl * rank, share)
+                right_ref[t] = dot(middle, block, NN)
+                high, low = split(inverse * scale)
+                stack = jnp.concatenate([high, high, low], axis=1)
+                basis_ref[t] = dot(stack, sample[t], NN)
+        when(all_own, next_layer(off) < owners, finish)
 
     for off in range(1, nl):
         core_copy(off).wait_send()

time: 56.8 us -> 59.8 us (1.053)
  Pallas kernels: 52.7 us -> 55.7 us
    pallas_call x1, Pallas kernels: 52.7 us -> 55.7 us  [local(): pl.pallas_call(functools.partial(kernel, nl, nc), out_shape=(out, out), i...]
where the time goes in v3:
time: 59.8 us; the launch traced here: 59.7 us
  Pallas kernels  55.7 us (93%)
  local copies, waits for them, and re-layouts  3.32 us (6%)
  between operations  0.65 us (1%)
    pallas_call x1, Pallas kernels, local(): pl.pallas_call(functools.partial(kernel, nl, nc), out_shape=(out, out), i...  55.7 us
    unnamed x4, local copies, waits for them, and re-layouts  3.32 us

profile of v3, /device:TPU:0, one launch (start us, length us, event | category | flops | bytes accessed | tf_op | source)
XLA Modules:
  0.0 59.7 jit_solution(14374528065404101115)
XLA Ops:
  0.6 55.7 %shard_map.59 = (f32[8,64,512]{2,1,0:T(8,128)}, f32[8,64,512]{2,1,0:T(8,128)}) custom-call(s32[2,8]{1,0:T(2,128)} %bitcast.13, bf16[64,2048]{1,0:T(8,128)(2,1)} %bitcast.11, f32[64,64]{1,0:T(8,128)} %bitcast.12, bf16[8,64,2048]{2,1,0:T(8,128)(2,1)} %bitcast.8), custom_call_target="tpu_custom_call" | custom-call | tf_op jit(solution)/shard_map/pallas_call | solution.py:381
  56.3 0.0 copy-start
  56.4 2.4 %copy.8 = f32[512,8,64]{0,2,1:T(8,128)} copy(f32[512,8,64]{0,2,1:T(8,128)} %bitcast.10) | data formatting | bytes 2097152
  58.7 0.0 copy-done
  58.7 1.0 %copy.9 = f32[512,8,64]{0,2,1:T(8,128)} copy(f32[512,8,64]{0,2,1:T(8,128)S(1)} %bitcast.9) | data formatting | bytes 2097152
Async XLA Ops:
  56.3 2.4 %copy-start = (f32[8,64,512]{2,1,0:T(8,128)S(1)}, f32[8,64,512]{2,1,0:T(8,128)}, u32[]{:S(2)}) copy-start(f32[8,64,512]{2,1,0:T(8,128)} %get-tuple-element.5) | copy-start | bytes 3145732

commit v4 on v2

--- a/solution.py
+++ b/solution.py
@@ -260,19 +260,15 @@
         gram_out[to, :, slot * rank : (slot + 1) * rank] = (
             product[:rank, :rank] + product[rank:, rank:]
             + (product[:rank, rank:] + product[rank:, :rank]))
-    for off in range(1, nl):
-        def send_gram(off=off):
-            exchange(lambda k: gram_out.at[k], lambda k: gram_in.at[k], s_gram, r_gram, off).start()
-        when(all_own, next_layer(off) < owners, send_gram)
-    for t in range(nt):
-        block = shared[tiles_ref[0, t]].reshape(nl * rank, share)
-        total = dot(sample[t, : 2 * rank], block, NT)
-        total = total[:rank] + total[rank:]
-        proj_out[t // per, t % per] = total.astype(jnp.bfloat16)
-    for off in range(1, nl):
-        def send_proj(off=off):
-            exchange(lambda k: proj_out.at[k], lambda k: proj_in.at[k], s_proj, r_proj, off).start()
-        when(all_own, next_layer(off) < owners, send_proj)
+        total = dot(both, block, NT)
+        proj_out[to, slot] = (total[:rank] + total[rank:]).astype(jnp.bfloat16)
+        if slot == per - 1:
+            @pl.when(l != to)
+            def send_sums(to=to):
+                remote(gram_out.at[to], gram_in.at[l], s_gram.at[to], r_gram.at[l],
+                       at_layer(to)).start()
+                remote(proj_out.at[to], proj_in.at[l], s_proj.at[to], r_proj.at[l],
+                       at_layer(to)).start()
 
     def own_tiles():
         gram = gram_out[l]

time: 56.8 us -> 59.7 us (1.051)
  Pallas kernels: 52.7 us -> 55.5 us
    pallas_call x1, Pallas kernels: 52.7 us -> 55.5 us  [local(): pl.pallas_call(functools.partial(kernel, nl, nc), out_shape=(out, out), i...]
where the time goes in v4:
time: 59.7 us; the launch traced here: 59.5 us
  Pallas kernels  55.5 us (93%)
  local copies, waits for them, and re-layouts  3.32 us (6%)
  between operations  0.65 us (1%)
    pallas_call x1, Pallas kernels, local(): pl.pallas_call(functools.partial(kernel, nl, nc), out_shape=(out, out), i...  55.5 us
    unnamed x4, local copies, waits for them, and re-layouts  3.32 us

profile of v4, /device:TPU:0, one launch (start us, length us, event | category | flops | bytes accessed | tf_op | source)
XLA Modules:
  0.0 59.5 jit_solution(1417582225512451534)
XLA Ops:
  0.6 55.5 %shard_map.59 = (f32[8,64,512]{2,1,0:T(8,128)}, f32[8,64,512]{2,1,0:T(8,128)}) custom-call(s32[2,8]{1,0:T(2,128)} %bitcast.13, bf16[64,2048]{1,0:T(8,128)(2,1)} %bitcast.11, f32[64,64]{1,0:T(8,128)} %bitcast.12, bf16[8,64,2048]{2,1,0:T(8,128)(2,1)} %bitcast.8), custom_call_target="tpu_custom_call" | custom-call | tf_op jit(solution)/shard_map/pallas_call | solution.py:373
  56.2 0.0 copy-start
  56.2 2.4 %copy.8 = f32[512,8,64]{0,2,1:T(8,128)} copy(f32[512,8,64]{0,2,1:T(8,128)} %bitcast.10) | data formatting | bytes 2097152
  58.5 0.0 copy-done
  58.5 1.0 %copy.9 = f32[512,8,64]{0,2,1:T(8,128)} copy(f32[512,8,64]{0,2,1:T(8,128)S(1)} %bitcast.9) | data formatting | bytes 2097152
Async XLA Ops:
  56.2 2.4 %copy-start = (f32[8,64,512]{2,1,0:T(8,128)S(1)}, f32[8,64,512]{2,1,0:T(8,128)}, u32[]{:S(2)}) copy-start(f32[8,64,512]{2,1,0:T(8,128)} %get-tuple-element.5) | copy-start | bytes 3145732

commit v5 on v2

--- a/solution.py
+++ b/solution.py
@@ -307,24 +307,28 @@
 
     when(all_own, l < owners, own_tiles)
 
-    for off in range(1, nl):
-        def take_inverse(off=off):
-            arrival(lambda k: inv.at[k], s_inv, r_inv, next_layer(off)).wait_recv()
-        when(all_own, next_layer(off) < owners, take_inverse)
     scale = math.sqrt(order)
-    for t in range(nt):
-        slot = t % per
-        inverse = inv[t // per][:, slot * rank : (slot + 1) * rank]
-        high, low = split(inverse * scale)
-        stack = jnp.concatenate([high, high, low], axis=1)
-        basis_ref[t] = dot(stack, sample[t], NN)
-    for off in range(1, nl):
-        def take_second(off=off):
-            arrival(lambda k: second.at[k], s_second, r_second, next_layer(off)).wait_recv()
-        when(all_own, next_layer(off) < owners, take_second)
-    for t in range(nt):
-        block = shared[tiles_ref[1, t]].reshape(nl * rank, share)
-        right_ref[t] = dot(second[t // per, t % per], block, NN)
+    for off in range(nl):
+        def finish_basis(off=off):
+            k = next_layer(off)
+            if off > 0:
+                arrival(lambda k: inv.at[k], s_inv, r_inv, k).wait_recv()
+            for slot in range(per):
+                t = k * per + slot
+                high, low = split(inv[k][:, slot * rank : (slot + 1) * rank] * scale)
+                stack = jnp.concatenate([high, high, low], axis=1)
+                basis_ref[t] = dot(stack, sample[t], NN)
+        when(all_own, next_layer(off) < owners, finish_basis)
+    for off in range(nl):
+        def finish_right(off=off):
+            k = next_layer(off)
+            if off > 0:
+                arrival(lambda k: second.at[k], s_second, r_second, k).wait_recv()
+            for slot in range(per):
+                t = k * per + slot
+                block = shared[tiles_ref[1, t]].reshape(nl * rank, share)
+                right_ref[t] = dot(second[k, slot], block, NN)
+        when(all_own, next_layer(off) < owners, finish_right)
 
     for off in range(1, nl):
         core_copy(off).wait_send()

time: 56.8 us -> 57 us (level)
  no operation moved by 1% of the time
where the time goes in v5:
time: 57 us; the launch traced here: 56.8 us
  Pallas kernels  52.8 us (93%)
  local copies, waits for them, and re-layouts  3.32 us (6%)
  between operations  0.65 us (1%)
    pallas_call x1, Pallas kernels, local(): pl.pallas_call(functools.partial(kernel, nl, nc), out_shape=(out, out), i...  52.8 us
    unnamed x4, local copies, waits for them, and re-layouts  3.32 us

profile of v5, /device:TPU:0, one launch (start us, length us, event | category | flops | bytes accessed | tf_op | source)
XLA Modules:
  0.0 56.8 jit_solution(8829889356129363365)
XLA Ops:
  0.6 52.8 %shard_map.59 = (f32[8,64,512]{2,1,0:T(8,128)}, f32[8,64,512]{2,1,0:T(8,128)}) custom-call(s32[2,8]{1,0:T(2,128)} %bitcast.13, bf16[64,2048]{1,0:T(8,128)(2,1)} %bitcast.11, f32[64,64]{1,0:T(8,128)} %bitcast.12, bf16[8,64,2048]{2,1,0:T(8,128)(2,1)} %bitcast.8), custom_call_target="tpu_custom_call" | custom-call | tf_op jit(solution)/shard_map/pallas_call | solution.py:381
  53.5 0.0 copy-start
  53.5 2.4 %copy.8 = f32[512,8,64]{0,2,1:T(8,128)} copy(f32[512,8,64]{0,2,1:T(8,128)} %bitcast.10) | data formatting | bytes 2097152
  55.8 0.0 copy-done
  55.8 1.0 %copy.9 = f32[512,8,64]{0,2,1:T(8,128)} copy(f32[512,8,64]{0,2,1:T(8,128)S(1)} %bitcast.9) | data formatting | bytes 2097152
Async XLA Ops:
  53.5 2.4 %copy-start = (f32[8,64,512]{2,1,0:T(8,128)S(1)}, f32[8,64,512]{2,1,0:T(8,128)}, u32[]{:S(2)}) copy-start(f32[8,64,512]{2,1,0:T(8,128)} %get-tuple-element.5) | copy-start | bytes 3145732

commit v6 on v2

--- a/solution.py
+++ b/solution.py
@@ -18,7 +18,7 @@
     return lax.dot_general(a, b, dims, precision=precision, preferred_element_type=jnp.float32)
 
 
-def invert_factor(gram, rank, count, width=4, depth=8):
+def invert_factor(gram, rank, count, width=8, depth=8):
     lanes = gram.shape[1]
     row = lax.broadcasted_iota(jnp.int32, gram.shape, 0)
     lane = lax.broadcasted_iota(jnp.int32, gram.shape, 1)

time: 56.8 us -> 56.8 us (level)
  no operation moved by 1% of the time
where the time goes in v6:
time: 56.8 us; the launch traced here: 56.7 us
  Pallas kernels  52.7 us (93%)
  local copies, waits for them, and re-layouts  3.32 us (6%)
  between operations  0.65 us (1%)
    pallas_call x1, Pallas kernels, local(): pl.pallas_call(functools.partial(kernel, nl, nc), out_shape=(out, out), i...  52.7 us
    unnamed x4, local copies, waits for them, and re-layouts  3.32 us

profile of v6, /device:TPU:0, one launch (start us, length us, event | category | flops | bytes accessed | tf_op | source)
XLA Modules:
  0.0 56.7 jit_solution(7963994327815246533)
XLA Ops:
  0.6 52.7 %shard_map.59 = (f32[8,64,512]{2,1,0:T(8,128)}, f32[8,64,512]{2,1,0:T(8,128)}) custom-call(s32[2,8]{1,0:T(2,128)} %bitcast.13, bf16[64,2048]{1,0:T(8,128)(2,1)} %bitcast.11, f32[64,64]{1,0:T(8,128)} %bitcast.12, bf16[8,64,2048]{2,1,0:T(8,128)(2,1)} %bitcast.8), custom_call_target="tpu_custom_call" | custom-call | tf_op jit(solution)/shard_map/pallas_call | solution.py:377
  53.3 0.0 copy-start
  53.3 2.4 %copy.8 = f32[512,8,64]{0,2,1:T(8,128)} copy(f32[512,8,64]{0,2,1:T(8,128)} %bitcast.10) | data formatting | bytes 2097152
  55.7 0.0 copy-done
  55.7 1.0 %copy.9 = f32[512,8,64]{0,2,1:T(8,128)} copy(f32[512,8,64]{0,2,1:T(8,128)S(1)} %bitcast.9) | data formatting | bytes 2097152
Async XLA Ops:
  53.3 2.4 %copy-start = (f32[8,64,512]{2,1,0:T(8,128)S(1)}, f32[8,64,512]{2,1,0:T(8,128)}, u32[]{:S(2)}) copy-start(f32[8,64,512]{2,1,0:T(8,128)} %get-tuple-element.5) | copy-start | bytes 3145732
